TPU v7x, 32 devices: a whole 2x2x4 slice. The times are simulated.
32 devices in a mesh: mode: 4 (over x, core), batch: 4 (over z), cores: 2 (over y).
Axes of the slice: x: 2, y: 2, z: 4, core: 2. Of those that a mesh axis runs over, the one named last changes fastest.
Arguments:
- fields: bfloat16 [4, 20, 1024, 1024], P('batch', None, ('mode', 'cores')), may hold values from -6 to 6
- lift_weight: bfloat16 [20, 128], replicated, may hold values from -1.25 to 1.25
- lift_bias: float32 [128], replicated, may hold values from -3 to 3
- first_core: bfloat16 [128, 32, 32], P('batch'), may hold values from -1 to 1
- second_core: bfloat16 [128, 32, 32], P(('mode', 'cores')), may hold values from -1 to 1
- input_core: bfloat16 [128, 32, 32], P('batch'), may hold values from -0.09375 to 0.09375
- output_core: bfloat16 [128, 2, 32, 32], P('batch'), may hold values from -3 to 3
- skip_weight: bfloat16 [128, 128], replicated, may hold values from -0.5 to 0.5
- skip_bias: float32 [128], replicated, may hold values from -3 to 3
- out_weight: bfloat16 [128, 20], replicated, may hold values from -0.5 to 0.5
- out_bias: float32 [20], replicated, may hold values from -3 to 3
Outputs:
- updated: bfloat16 [4, 20, 1024, 1024], P('batch', None, ('mode', 'cores'))
All inputs are finite; a program needn't handle non-finite values.
Results may differ from a plain program's by a relative error of at most 0.012.
Values may be sent and summed in bfloat16 or wider, within the bound.
A program may use at most 256 MiB of HBM per device.

v0:
```python
import math
import jax
import jax.numpy as jnp
from jax import lax
from jax.sharding import PartitionSpec as P

NX = 1024
NY = 1024
MX = 128
MY = 128
TWO_PI = 2.0 * math.pi


def wave_pair(waves, points, length):
    phase_step = waves[:, None] * points[None, :] % length
    angles = phase_step.astype(jnp.float32) * (TWO_PI / length)
    return (jnp.cos(angles), jnp.sin(angles))


def width_forward(length, wave_count):
    points = jnp.arange(length, dtype=jnp.int32)
    waves = jnp.arange(wave_count, dtype=jnp.int32)
    cosines, sine_part = wave_pair(points, waves, length)
    stacked = jnp.stack([cosines, -sine_part], axis=1) / math.sqrt(length)
    return stacked.astype(jnp.bfloat16)


def height_forward(row_index, wave_count, length):
    waves = jnp.arange(wave_count, dtype=jnp.int32) - wave_count // 2
    cosines, sine_part = wave_pair(waves, row_index, length)
    upper = jnp.stack([cosines, sine_part], axis=1)
    lower = jnp.stack([-sine_part, cosines], axis=1)
    return (jnp.stack([upper, lower], axis=0) / math.sqrt(length)).astype(jnp.bfloat16)


def height_inverse(row_index, wave_count, length):
    waves = jnp.arange(wave_count, dtype=jnp.int32) - wave_count // 2
    cosines, sine_part = wave_pair(row_index, waves, length)
    upper = jnp.stack([cosines, -sine_part], axis=1)
    lower = jnp.stack([sine_part, cosines], axis=1)
    return (jnp.stack([upper, lower], axis=0) / math.sqrt(length)).astype(jnp.bfloat16)


def width_inverse(waves, length):
    points = jnp.arange(length, dtype=jnp.int32)
    cosines, sine_part = wave_pair(waves, points, length)
    weight = jnp.where(waves == 0, 1.0, 2.0).astype(jnp.float32)[:, None]
    stacked = jnp.stack([cosines * weight, -sine_part * weight], axis=0) / math.sqrt(length)
    return stacked.astype(jnp.bfloat16)


def bias_modes(lift_bias, wave_index, length):
    real_row = (
        jnp.where(wave_index == 0, 1.0, 0.0).astype(jnp.float32)[:, None]
        * (math.sqrt(length) * lift_bias)[None, :]
    )
    return jnp.stack([real_row, jnp.zeros_like(real_row)], axis=0)


def lift_modes(modes, lift_weight, lift_bias, wave_index):
    lifted_modes = jnp.einsum(
        "fabpmv,vc->fabpmc", modes, lift_weight, preferred_element_type=jnp.float32
    )
    return (lifted_modes + bias_modes(lift_bias, wave_index, NY)).astype(jnp.bfloat16)


def grid_rows(stored, row_count, holder_count):
    return stored % row_count * holder_count + stored // row_count


def shards(
    fields,
    lift_weight,
    lift_bias,
    first_core,
    second_core,
    input_core,
    output_core,
    skip_weight,
    skip_bias,
    out_weight,
    out_bias,
):
    mode_count = lax.axis_size("mode")
    core_count = lax.axis_size("cores")
    row_count = fields.shape[2]
    block_size = second_core.shape[0]
    block_start = (lax.axis_index("mode") * core_count + lax.axis_index("cores")) * block_size
    local_waves = block_start + jnp.arange(block_size, dtype=jnp.int32)
    lifted = (
        jnp.einsum("fvxy,vc->fxyc", fields, lift_weight, preferred_element_type=jnp.float32)
        + lift_bias
    ).astype(jnp.bfloat16)
    field_modes = jnp.einsum(
        "fvxy,ypk->fxpkv", fields, width_forward(NY, MY), preferred_element_type=jnp.float32
    ).astype(jnp.bfloat16)
    field_modes = field_modes[:, None]
    gathered = (
        lax.all_gather(first_core, "batch", axis=0, tiled=True),
        lax.all_gather(input_core, "batch", axis=0, tiled=True),
        lax.all_gather(output_core, "batch", axis=0, tiled=True),
    )
    first_whole, input_whole, output_whole = gathered
    mode_factor = jnp.einsum(
        "kab,mbd->kmad", first_whole, second_core, preferred_element_type=jnp.float32
    ).astype(jnp.bfloat16)
    arrived = lax.all_to_all(
        field_modes, ("mode", "cores"), split_axis=4, concat_axis=2, tiled=True
    )
    rows_held = jnp.arange(NX, dtype=jnp.int32)[None, :]
    by_mode = lift_modes(arrived, lift_weight, lift_bias, local_waves)
    lead_rows = rows_held.shape[0]
    side_rows = rows_held.shape[1]
    flat_rows = grid_rows(rows_held.reshape(-1), row_count, mode_count * core_count)
    height_table = height_forward(flat_rows, MX, NX).reshape(2, MX, 2, lead_rows, side_rows)
    spectrum = jnp.einsum(
        "qkpab,fabpmc->fqkmc", height_table, by_mode, preferred_element_type=jnp.float32
    ).astype(jnp.bfloat16)
    projected = jnp.einsum(
        "fqkmc,cbe->fqkmbe", spectrum, input_whole, preferred_element_type=jnp.float32
    ).astype(jnp.bfloat16)
    carried = jnp.einsum(
        "kmab,fqkmbe->fqkmae", mode_factor, projected, preferred_element_type=jnp.float32
    ).astype(jnp.bfloat16)
    traced = jnp.einsum(
        "fqkmae,osea->fqkmso", carried, output_whole, preferred_element_type=jnp.float32
    )
    real_part = traced[:, 0, :, :, 0, :] - traced[:, 1, :, :, 1, :]
    imaginary = traced[:, 0, :, :, 1, :] + traced[:, 1, :, :, 0, :]
    mixed_modes = jnp.stack([real_part, imaginary], axis=1).astype(jnp.bfloat16)
    height_back = height_inverse(flat_rows, MX, NX).reshape(2, lead_rows, side_rows, 2, MX)
    col_modes = jnp.einsum(
        "pabqk,fqkmc->fabpmc", height_back, mixed_modes, preferred_element_type=jnp.float32
    ).astype(jnp.bfloat16)
    returned = lax.all_to_all(col_modes, ("mode", "cores"), split_axis=2, concat_axis=4, tiled=True)
    waves_held = jnp.arange(MY, dtype=jnp.int32)
    width_back = width_inverse(waves_held, NY)
    spatial = jnp.einsum(
        "fxpmc,pmy->fxyc", returned[:, 0], width_back, preferred_element_type=jnp.float32
    )
    skip_term = jnp.einsum("fxyc,cd->fxyd", lifted, skip_weight, preferred_element_type=jnp.float32)
    active = jax.nn.gelu(spatial + skip_term + skip_bias, approximate=False).astype(jnp.bfloat16)
    result = (
        jnp.einsum("fxyc,cv->fvxy", active, out_weight, preferred_element_type=jnp.float32)
        + out_bias[:, None, None]
    )
    return result.astype(jnp.bfloat16)


def solution(mesh):
    placed = (
        P("batch", None, ("mode", "cores"), None),
        P(),
        P(),
        P("batch", None, None),
        P(("mode", "cores"), None, None),
        P("batch", None, None),
        P("batch", None, None, None),
        P(),
        P(),
        P(),
        P(),
    )
    return jax.shard_map(
        shards,
        mesh=mesh,
        in_specs=placed,
        out_specs=P("batch", None, ("mode", "cores"), None),
        check_vma=False,
    )
```

profile of v0, /device:TPU:0, one launch (start us, length us, event | category | flops | bytes accessed | tf_op | source)
XLA Modules:
  0.0 632.1 jit_solution(4444873286141601486)
XLA Ops:
  0.0 2.1 sine_negate_fusion
  2.1 4.1 fusion.36
  6.1 2.4 copy.49
  8.6 5.2 all-to-all-start
  14.4 1.8 copy.59
  16.3 22.9 %all_gather.10 = bf16[128,32,32]{2,1,0:T(8,128)(2,1)S(1)} all-gather(bf16[32,32,32]{2,1,0:T(8,128)(2,1)} %param.14), channel_id=1, replica_groups=mesh['mode'=4,'batch'=4,'cores'=2] {'batch'}, dimensions={0}, use_global_device_ids=true | all-gather | bytes 327680 | tf_op jit(solution)/shard_map/all_gather | solution.py:99
  39.2 3.3 convert_bitcast_fusion.1
  42.5 23.0 %copy.75 = bf16[128,16,32,32,1]{3,2,4,1,0:T(8,128)(2,1)} copy(bf16[128,16,32,32,1]{0,3,2,1,4:T(8,128)(2,1)} %convert_bitcast_fusion.1) | data formatting | bytes 8388608 | tf_op jit(solution)/shard_map/convert_element_type | solution.py:106
  65.6 24.2 %all_gather.9 = bf16[128,32,32]{2,1,0:T(8,128)(2,1)} all-gather(bf16[32,32,32]{2,1,0:T(8,128)(2,1)} %param.16), channel_id=1, replica_groups=mesh['mode'=4,'batch'=4,'cores'=2] {'batch'}, dimensions={0}, use_global_device_ids=true | all-gather | bytes 327680 | tf_op jit(solution)/shard_map/all_gather | solution.py:100
  89.8 2.1 fusion.87
  92.0 1.6 maximum_bitcast_fusion
  93.5 2.1 fusion.92
  95.6 1.6 maximum_bitcast_fusion.3
  97.2 36.8 %all_gather.11 = bf16[128,2,32,32]{2,0,3,1:T(8,128)(2,1)} all-gather(bf16[32,2,32,32]{2,0,3,1:T(8,128)(2,1)S(1)} %copy.59), channel_id=1, replica_groups=mesh['mode'=4,'batch'=4,'cores'=2] {'batch'}, dimensions={0}, use_global_device_ids=true | all-gather | bytes 655360 | tf_op jit(solution)/shard_map/all_gather | solution.py:101
  134.1 0.8 copy.118
  134.9 0.9 reshape.755
  135.8 8.7 %fusion.39 = bf16[2,128,16,128,1]{1,3,0,2,4:T(8,128)(2,1)S(1)} fusion(f32[2,16,128]{2,0,1:T(2,128)S(1)} %stack.59, bf16[1024,2,16,20]{0,2,3,1:T(8,128)(2,1)S(1)} %reshape.755, f32[1,128,2,1024]{3,1,2,0:T(8,128)} %get-tuple-element.6, f32[1,128,2,1024]{3,1,2,0:T(8,128)} %get-tuple-element.5, bf16[20,128]{1,0:T(8,128)(2,1)} %param.12), kind=kOutput, calls=%fused_computation.50 | convolution fusion | flops 2325741568 | bytes 4477952 | tf_op jit(solution)/shard_map/qkpab,fabpmc->fqkmc/dot_general | solution.py:116
  144.5 6.9 %convolution_convert_fusion = bf16[2,128,16,32,32]{1,4,3,2,0:T(8,128)(2,1)} fusion(bf16[128,32,32,1,1]{2,1,0,4,3:T(8,128)(2,1)} %bitcast.201, bf16[2,128,16,128,1]{1,3,0,2,4:T(8,128)(2,1)S(1)} %fusion.39), kind=kOutput, calls=%fused_computation.36 | convolution fusion | flops 1077936128 | bytes 9699328 | tf_op jit(solution)/shard_map/fqkmc,cbe->fqkmbe/dot_general | solution.py:119
  151.4 54.9 %copy.57 = bf16[2,128,16,32,32]{3,4,0,2,1:T(8,128)(2,1)} copy(bf16[2,128,16,32,32]{1,4,3,2,0:T(8,128)(2,1)} %convolution_convert_fusion) | data formatting | bytes 16777216 | tf_op jit(solution)/shard_map/convert_element_type | solution.py:121
  206.3 28.3 %convert_bitcast_fusion = bf16[2,128,16,32,32,1]{3,4,0,2,1,5:T(8,128)(2,1)} fusion(bf16[2,128,16,32,32]{3,4,0,2,1:T(8,128)(2,1)} %copy.57, bf16[128,16,32,32,1]{3,2,4,1,0:T(8,128)(2,1)} %copy.75), kind=kOutput, calls=%fused_computation.26 | convolution fusion | flops 272629760 | bytes 20971520 | tf_op jit(solution)/shard_map/kmab,fqkmbe->fqkmae/dot_general | solution.py:122
  234.6 47.5 %copy.76 = bf16[2,128,16,32,32,1]{1,4,3,5,2,0:T(8,128)(2,1)} copy(bf16[2,128,16,32,32,1]{3,4,0,2,1,5:T(8,128)(2,1)} %convert_bitcast_fusion) | data formatting | bytes 16777216 | tf_op jit(solution)/shard_map/reshape.14
  282.1 12.4 %convolution_bitcast_fusion = f32[1,2,128,16,2,128]{5,2,4,3,1,0:T(8,128)S(1)} fusion(bf16[2,128,16,32,32,1]{1,4,3,5,2,0:T(8,128)(2,1)} %copy.76, bf16[128,2,32,32]{2,0,3,1:T(8,128)(2,1)} %all_gather.11), kind=kOutput, calls=%fused_computation.40 | convolution fusion | flops 2147483648 | bytes 13107200 | tf_op jit(solution)/shard_map/fqkmae,osea->fqkmso/dot_general | solution.py:125
  294.8 5.6 fusion.21
  300.4 21.3 %copy.65 = bf16[1,1,1024,2,16,128]{5,3,4,1,0,2:T(2,128)(2,1)} copy(bf16[1,1,1024,2,16,128]{2,5,3,4,1,0:T(8,128)(2,1)} %fusion.21) | data formatting | bytes 16777216 | tf_op jit(solution)/shard_map/convert_element_type | solution.py:134
  321.7 5.1 all-to-all-start.1
  326.8 2.1 cosine_multiply_fusion
  328.9 27.3 %fusion.19 = f32[128,1024,128]{2,1,0:T(8,128)} fusion(bf16[20,128,1024]{2,1,0:T(8,128)(2,1)} %bitcast.198, bf16[20,128]{1,0:T(8,128)(2,1)S(1)} %copy-done.4), kind=kOutput, calls=%fused_computation.33 | convolution fusion | flops 671088640 | bytes 72356864 | tf_op jit(solution)/shard_map/fvxy,vc->fxyc/dot_general | solution.py:91
  356.2 63.7 %all-to-all-done.1 = bf16[1,1,1024,2,16,128]{5,3,4,1,0,2:T(2,128)(2,1)} async-done(((bf16[1,1,1024,2,16,128]{5,3,4,1,0,2:T(2,128)(2,1)}), bf16[1,1,1024,2,16,128]{5,3,4,1,0,2:T(2,128)(2,1)}, u32[]{:S(2)}, u32[]{:S(2)}) %all-to-all-start.1) | async-done | bytes 8388640 | tf_op jit(solution)/shard_map/all_to_all | solution.py:135
  420.0 9.1 %copy.66 = bf16[1,1,8,128,2,16,128]{6,5,2,4,3,1,0:T(8,128)(2,1)} copy(bf16[1,1,8,128,2,16,128]{6,4,5,3,2,1,0:T(2,128)(2,1)} %bitcast.50) | data formatting | bytes 16777216 | tf_op jit(solution)/shard_map/all_to_all | solution.py:135
  429.1 26.7 %fusion.75 = f32[1024,128,128,1]{2,0,3,1:T(8,128)} fusion(bf16[128,2,128,128]{3,2,1,0:T(8,128)(2,1)} %bitcast.197, f32[1,128,1024]{1,2,0:T(8,128)S(1)} %get-tuple-element.16, f32[1,128,1024]{1,2,0:T(8,128)S(1)} %get-tuple-element.15), kind=kOutput, calls=%fused_computation.106 | convolution fusion | flops 8590721024 | bytes 76546048 | tf_op jit(solution)/shard_map/fxpmc,pmy->fxyc/dot_general | solution.py:138
  455.8 167.8 %fusion.18 = bf16[1,20,128,1024]{3,1,2,0:T(8,128)(2,1)} fusion(f32[20]{0:T(128)S(1)} %copy-done.7, f32[128]{0:T(128)S(1)} %copy-done.8, f32[1024,128,128,1]{2,0,3,1:T(8,128)} %fusion.75, f32[128,1024,128]{2,1,0:T(8,128)} %fusion.19, f32[128]{0:T(128)S(1)} %copy-done.9, bf16[128,128]{1,0:T(8,128)(2,1)S(1)} %copy-done.5, bf16[128,20]{0,1:T(8,128)(2,1)S(1)} %copy-done.6), kind=kOutput, calls=%fused_computation.32 | convolution fusion | flops 6128926720 | bytes 139499600 | tf_op jit(solution)/shard_map/fxyc,cv->fvxy/dot_general | solution.py:144
  623.6 8.1 %copy.68 = bf16[1,20,128,1024]{3,2,1,0:T(8,128)(2,1)} copy(bf16[1,20,128,1024]{3,1,2,0:T(8,128)(2,1)} %fusion.18) | data formatting | bytes 10485760 | tf_op jit(solution)/shard_map/convert_element_type | solution.py:147
  (30 shorter events, 1.0 us)
Async XLA Ops:
  0.0 39.2 %copy-start = (bf16[16,32,32]{2,1,0:T(8,128)(2,1)S(1)}, bf16[16,32,32]{2,1,0:T(8,128)(2,1)}, u32[]{:S(2)}) copy-start(bf16[16,32,32]{2,1,0:T(8,128)(2,1)} %param.15) | copy-start | bytes 98308
  8.6 125.5 %all-to-all-start = ((bf16[1,1,128,2,128,20]{2,3,5,1,0,4:T(2,128)(2,1)}), bf16[1,1,128,2,128,20]{2,3,5,1,0,4:T(2,128)(2,1)S(1)}, u32[]{:S(2)}, u32[]{:S(2)}) async-start(bf16[1,1,128,2,128,20]{2,3,5,1,0,4:T(2,128)(2,1)} %copy.49), calls=%async_computation | async-start | bytes 2621440 | tf_op jit(solution)/shard_map/all_to_all | solution.py:107
  234.6 60.2 %copy-start.2 = (f32[1,1024,2,128]{1,3,2,0:T(8,128)S(1)}, f32[1,1024,2,128]{1,3,2,0:T(8,128)}, u32[]{:S(2)}) copy-start(f32[1,1024,2,128]{1,3,2,0:T(8,128)} %get-tuple-element.7) | copy-start | bytes 3145732
  234.6 60.2 %copy-start.3 = (f32[1,1024,2,128]{1,3,2,0:T(8,128)S(1)}, f32[1,1024,2,128]{1,3,2,0:T(8,128)}, u32[]{:S(2)}) copy-start(f32[1,1024,2,128]{1,3,2,0:T(8,128)} %get-tuple-element.8) | copy-start | bytes 3145732
  234.6 94.3 %copy-start.4 = (bf16[20,128]{1,0:T(8,128)(2,1)S(1)}, bf16[20,128]{1,0:T(8,128)(2,1)}, u32[]{:S(2)}) copy-start(bf16[20,128]{1,0:T(8,128)(2,1)} %param.12) | copy-start | bytes 15364
  321.7 98.3 %all-to-all-start.1 = ((bf16[1,1,1024,2,16,128]{5,3,4,1,0,2:T(2,128)(2,1)}), bf16[1,1,1024,2,16,128]{5,3,4,1,0,2:T(2,128)(2,1)}, u32[]{:S(2)}, u32[]{:S(2)}) async-start(bf16[1,1,1024,2,16,128]{5,3,4,1,0,2:T(2,128)(2,1)} %copy.65), calls=%async_computation.1 | async-start | bytes 16777216 | tf_op jit(solution)/shard_map/all_to_all | solution.py:135
  356.2 99.6 %copy-start.5 = (bf16[128,128]{1,0:T(8,128)(2,1)S(1)}, bf16[128,128]{1,0:T(8,128)(2,1)}, u32[]{:S(2)}) copy-start(bf16[128,128]{1,0:T(8,128)(2,1)} %param.18) | copy-start | bytes 98308
  356.2 99.6 %copy-start.6 = (bf16[128,20]{0,1:T(8,128)(2,1)S(1)}, bf16[128,20]{0,1:T(8,128)(2,1)}, u32[]{:S(2)}) copy-start(bf16[128,20]{0,1:T(8,128)(2,1)} %param.20) | copy-start | bytes 15364
  356.2 99.6 %copy-start.7 = (f32[20]{0:T(128)S(1)}, f32[20]{0:T(128)}, u32[]{:S(2)}) copy-start(f32[20]{0:T(128)} %param.21) | copy-start | bytes 244
  356.2 99.6 %copy-start.8 = (f32[128]{0:T(128)S(1)}, f32[128]{0:T(128)}, u32[]{:S(2)}) copy-start(f32[128]{0:T(128)} %param.19) | copy-start | bytes 1540
  356.2 99.6 %copy-start.9 = (f32[128]{0:T(128)S(1)}, f32[128]{0:T(128)}, u32[]{:S(2)}) copy-start(f32[128]{0:T(128)} %param.13) | copy-start | bytes 1540
  455.8 175.9 %copy-start.1 = (bf16[16,32,32]{2,1,0:T(8,128)(2,1)S(1)}, bf16[16,32,32]{2,1,0:T(8,128)(2,1)}, u32[]{:S(2)}) copy-start(bf16[16,32,32]{2,1,0:T(8,128)(2,1)} %param.15) | copy-start | bytes 98308
where the time goes:
time: 640 us; the launch traced here: 632 us
  matrix products  291 us (45%)
  local copies, waits for them, and re-layouts  170 us (27%)
  blocking collectives  83.9 us (13%)
  waiting for transfers between devices  63.8 us (10%)
  other arithmetic  12.5 us (2%)
  starting transfers between devices  10.3 us (2%)
    dot_general x1, matrix products, shards(): jnp.einsum('fxyc,cv->fvxy', active, out_weight, preferred_element_type=jn...  168 us
    all_to_all x1, waiting for transfers between devices, shards(): lax.all_to_all(col_modes, ('mode', 'cores'), split_axis=2, concat_axis=4,...  63.7 us
    convert_element_type x1, local copies, waits for them, and re-layouts, shards(): projected = jnp.einsum('fqkmc,cbe->fqkmbe', spectrum, input_whole, prefer...  54.9 us
    another operation x2, local copies, waits for them, and re-layouts  48.3 us
    all_gather x1, blocking collectives, shards(): lax.all_gather(output_core, 'batch', axis=0, tiled=True)  36.8 us
    dot_general x1, matrix products, shards(): jnp.einsum('kmab,fqkmbe->fqkmae', mode_factor, projected, preferred_eleme...  28.3 us
    dot_general x1, matrix products, shards(): jnp.einsum('fvxy,vc->fxyc', fields, lift_weight, preferred_element_type=j...  27.3 us
    dot_general x1, matrix products, shards(): jnp.einsum('fxpmc,pmy->fxyc', returned[:, 0], width_back, preferred_eleme...  26.7 us
  transfers between devices with their start and end apart: 2, of which 1 were waited for; matrix products, arithmetic and copies ran while one was open for 10% of the time, Pallas kernels for 0%

commit v1 on v0

--- a/solution.py
+++ b/solution.py
@@ -132,7 +132,15 @@
     col_modes = jnp.einsum(
         "pabqk,fqkmc->fabpmc", height_back, mixed_modes, preferred_element_type=jnp.float32
     ).astype(jnp.bfloat16)
-    returned = lax.all_to_all(col_modes, ("mode", "cores"), split_axis=2, concat_axis=4, tiled=True)
+    returned = jnp.concatenate(
+        jax.lax.all_to_all(
+            jnp.stack(jnp.split(col_modes, jax.lax.axis_size(("mode", "cores")), axis=2), 0),
+            ("mode", "cores"),
+            0,
+            0,
+        ),
+        axis=4,
+    )
     waves_held = jnp.arange(MY, dtype=jnp.int32)
     width_back = width_inverse(waves_held, NY)
     spatial = jnp.einsum(

time: 640 us -> 625 us (0.977)
  local copies, waits for them, and re-layouts: 170 us -> 162 us
    convert_element_type x1 -> x0, local copies, waits for them, and re-layouts: 21.3 us -> none  [shards(): col_modes = jnp.einsum('pabqk,fqkmc->fabpmc', height_back, mixed_modes, p...]
    another operation x2 -> x4, local copies, waits for them, and re-layouts: 48.3 us -> 62 us
    all_to_all x1 -> x0, local copies, waits for them, and re-layouts: 9.14 us -> none  [shards(): lax.all_to_all(col_modes, ('mode', 'cores'), split_axis=2, concat_axis=4,...]
    unnamed x21 -> x32, local copies, waits for them, and re-layouts: 1.87 us -> 10.9 us
  transfers between devices with their start and end apart: 2 -> 2, of which waited for: 1 -> 1; matrix products, arithmetic and copies ran while one was open for 10% -> 11% of each run, Pallas kernels for 0% -> 0%
where the time goes in v1:
time: 625 us; the launch traced here: 618 us
  matrix products  287 us (46%)
  local copies, waits for them, and re-layouts  162 us (26%)
  blocking collectives  81.4 us (13%)
  waiting for transfers between devices  63.8 us (10%)
  other arithmetic  12.5 us (2%)
  starting transfers between devices  10.3 us (2%)
    dot_general x1, matrix products, shards(): jnp.einsum('fxyc,cv->fvxy', active, out_weight, preferred_element_type=jn...  168 us
    all_to_all x1, waiting for transfers between devices, shards(): jax.lax.all_to_all(jnp.stack(jnp.split(col_modes, jax.lax.axis_size(('mod...  63.8 us
    another operation x3, local copies, waits for them, and re-layouts  60.7 us
    convert_element_type x1, local copies, waits for them, and re-layouts, shards(): projected = jnp.einsum('fqkmc,cbe->fqkmbe', spectrum, input_whole, prefer...  54.9 us
    all_gather x1, blocking collectives, shards(): lax.all_gather(output_core, 'batch', axis=0, tiled=True)  35.4 us
    dot_general x1, matrix products, shards(): jnp.einsum('kmab,fqkmbe->fqkmae', mode_factor, projected, preferred_eleme...  28.2 us
    dot_general x1, matrix products, shards(): jnp.einsum('fvxy,vc->fxyc', fields, lift_weight, preferred_element_type=j...  27.3 us
    dot_general x1, matrix products, shards(): jnp.einsum('fxpmc,pmy->fxyc', returned[:, 0], width_back, preferred_eleme...  26.6 us
  transfers between devices with their start and end apart: 2, of which 1 were waited for; matrix products, arithmetic and copies ran while one was open for 11% of the time, Pallas kernels for 0%

profile of v1, /device:TPU:0, one launch (start us, length us, event | category | flops | bytes accessed | tf_op | source)
XLA Modules:
  0.0 618.0 jit_solution(10670639023242473408)
XLA Ops:
  0.0 2.1 sine_negate_fusion
  2.1 4.1 fusion.36
  6.1 2.4 copy.48
  8.6 5.2 all-to-all-start
  14.4 1.8 copy.58
  16.3 22.9 %all_gather.10 = bf16[128,32,32]{2,1,0:T(8,128)(2,1)S(1)} all-gather(bf16[32,32,32]{2,1,0:T(8,128)(2,1)} %param.14), channel_id=1, replica_groups=mesh['mode'=4,'batch'=4,'cores'=2] {'batch'}, dimensions={0}, use_global_device_ids=true | all-gather | bytes 327680 | tf_op jit(solution)/shard_map/all_gather | solution.py:99
  39.2 3.3 convert_bitcast_fusion.1
  42.5 23.1 %copy.73 = bf16[128,16,32,32,1]{3,2,4,1,0:T(8,128)(2,1)} copy(bf16[128,16,32,32,1]{0,3,2,1,4:T(8,128)(2,1)} %convert_bitcast_fusion.1) | data formatting | bytes 8388608 | tf_op jit(solution)/shard_map/convert_element_type | solution.py:106
  65.6 23.1 %all_gather.9 = bf16[128,32,32]{2,1,0:T(8,128)(2,1)} all-gather(bf16[32,32,32]{2,1,0:T(8,128)(2,1)S(1)} %copy-done.5), channel_id=1, replica_groups=mesh['mode'=4,'batch'=4,'cores'=2] {'batch'}, dimensions={0}, use_global_device_ids=true | all-gather | bytes 327680 | tf_op jit(solution)/shard_map/all_gather | solution.py:100
  88.8 2.1 fusion.95
  90.9 1.6 maximum_bitcast_fusion
  92.4 2.1 fusion.100
  94.6 1.6 maximum_bitcast_fusion.3
  96.1 35.4 %all_gather.11 = bf16[128,2,32,32]{2,0,3,1:T(8,128)(2,1)} all-gather(bf16[32,2,32,32]{2,0,3,1:T(8,128)(2,1)S(1)} %copy.58), channel_id=1, replica_groups=mesh['mode'=4,'batch'=4,'cores'=2] {'batch'}, dimensions={0}, use_global_device_ids=true | all-gather | bytes 655360 | tf_op jit(solution)/shard_map/all_gather | solution.py:101
  133.2 8.7 %fusion.39 = bf16[2,128,16,128,1]{1,3,0,2,4:T(8,128)(2,1)S(1)} fusion(f32[2,16,128]{2,0,1:T(2,128)S(1)} %stack.86, bf16[1024,2,16,20]{0,2,3,1:T(8,128)(2,1)S(1)} %reshape.757, f32[1,128,2,1024]{3,1,2,0:T(8,128)} %get-tuple-element.6, f32[1,128,2,1024]{3,1,2,0:T(8,128)} %get-tuple-element.5, bf16[20,128]{1,0:T(8,128)(2,1)S(1)} %copy-done.6), kind=kOutput, calls=%fused_computation.50 | convolution fusion | flops 2325741568 | bytes 4477952 | tf_op jit(solution)/shard_map/qkpab,fabpmc->fqkmc/dot_general | solution.py:116
  141.9 6.9 %convolution_convert_fusion = bf16[2,128,16,32,32]{1,4,3,2,0:T(8,128)(2,1)} fusion(bf16[128,32,32,1,1]{2,1,0,4,3:T(8,128)(2,1)} %bitcast.231, bf16[2,128,16,128,1]{1,3,0,2,4:T(8,128)(2,1)S(1)} %fusion.39), kind=kOutput, calls=%fused_computation.36 | convolution fusion | flops 1077936128 | bytes 9699328 | tf_op jit(solution)/shard_map/fqkmc,cbe->fqkmbe/dot_general | solution.py:119
  148.9 54.9 %copy.56 = bf16[2,128,16,32,32]{3,4,0,2,1:T(8,128)(2,1)} copy(bf16[2,128,16,32,32]{1,4,3,2,0:T(8,128)(2,1)} %convolution_convert_fusion) | data formatting | bytes 16777216 | tf_op jit(solution)/shard_map/convert_element_type | solution.py:121
  203.8 28.2 %convert_bitcast_fusion = bf16[2,128,16,32,32,1]{3,4,0,2,1,5:T(8,128)(2,1)} fusion(bf16[2,128,16,32,32]{3,4,0,2,1:T(8,128)(2,1)} %copy.56, bf16[128,16,32,32,1]{3,2,4,1,0:T(8,128)(2,1)} %copy.73), kind=kOutput, calls=%fused_computation.26 | convolution fusion | flops 272629760 | bytes 20971520 | tf_op jit(solution)/shard_map/kmab,fqkmbe->fqkmae/dot_general | solution.py:122
  232.0 47.5 %copy.74 = bf16[2,128,16,32,32,1]{1,4,3,5,2,0:T(8,128)(2,1)} copy(bf16[2,128,16,32,32,1]{3,4,0,2,1,5:T(8,128)(2,1)} %convert_bitcast_fusion) | data formatting | bytes 16777216 | tf_op jit(solution)/shard_map/reshape.15
  279.5 11.9 %convolution_bitcast_fusion = f32[1,2,128,16,2,128]{5,2,4,3,1,0:T(8,128)S(1)} fusion(bf16[2,128,16,32,32,1]{1,4,3,5,2,0:T(8,128)(2,1)} %copy.74, bf16[128,2,32,32]{2,0,3,1:T(8,128)(2,1)S(1)} %copy-done.4), kind=kOutput, calls=%fused_computation.40 | convolution fusion | flops 2147483648 | bytes 13107200 | tf_op jit(solution)/shard_map/fqkmae,osea->fqkmso/dot_general | solution.py:125
  291.7 2.4 fusion.21
  294.0 1.3 fusion.55
  299.2 1.3 fusion.51
  303.0 1.3 fusion.48
  304.3 5.1 all-to-all-start.1
  309.5 2.1 cosine_multiply_fusion
  311.6 27.3 %fusion.19 = f32[128,1024,128]{2,1,0:T(8,128)} fusion(bf16[20,128,1024]{2,1,0:T(8,128)(2,1)} %bitcast.228, bf16[20,128]{1,0:T(8,128)(2,1)S(1)} %copy-done.6), kind=kOutput, calls=%fused_computation.33 | convolution fusion | flops 671088640 | bytes 72356864 | tf_op jit(solution)/shard_map/fvxy,vc->fxyc/dot_general | solution.py:91
  338.9 63.8 %all-to-all-done.1 = bf16[8,1,1,128,2,16,128]{3,6,4,5,2,1,0:T(8,128)(2,1)} async-done(((bf16[8,1,1,128,2,16,128]{3,6,4,5,2,1,0:T(8,128)(2,1)}), bf16[8,1,1,128,2,16,128]{3,6,4,5,2,1,0:T(8,128)(2,1)}, u32[]{:S(2)}, u32[]{:S(2)}) %all-to-all-start.1) | async-done | bytes 8388640 | tf_op jit(solution)/shard_map/all_to_all | solution.py:136
  402.6 12.4 %copy.64 = bf16[128,2,128,128]{3,2,1,0:T(8,128)(2,1)} copy(bf16[128,2,128,128]{0,3,1,2:T(8,128)(2,1)} %bitcast.60) | data formatting | bytes 16777216 | tf_op jit(solution)/shard_map/reshape.20
  415.1 26.6 %fusion.83 = f32[1024,128,128,1]{2,0,3,1:T(8,128)} fusion(bf16[128,2,128,128]{3,2,1,0:T(8,128)(2,1)} %copy.64, f32[1,128,1024]{1,2,0:T(8,128)S(1)} %get-tuple-element.16, f32[1,128,1024]{1,2,0:T(8,128)S(1)} %get-tuple-element.15), kind=kOutput, calls=%fused_computation.122 | convolution fusion | flops 8590721024 | bytes 76546048 | tf_op jit(solution)/shard_map/fxpmc,pmy->fxyc/dot_general | solution.py:146
  441.7 167.8 %fusion.18 = bf16[1,20,128,1024]{3,1,2,0:T(8,128)(2,1)} fusion(f32[20]{0:T(128)S(1)} %copy-done.9, f32[128]{0:T(128)S(1)} %copy-done.10, f32[1024,128,128,1]{2,0,3,1:T(8,128)} %fusion.83, f32[128,1024,128]{2,1,0:T(8,128)} %fusion.19, f32[128]{0:T(128)S(1)} %copy-done.11, bf16[128,128]{1,0:T(8,128)(2,1)S(1)} %copy-done.7, bf16[128,20]{0,1:T(8,128)(2,1)S(1)} %copy-done.8), kind=kOutput, calls=%fused_computation.32 | convolution fusion | flops 6128926720 | bytes 139499600 | tf_op jit(solution)/shard_map/fxyc,cv->fvxy/dot_general | solution.py:152
  609.5 8.1 %copy.66 = bf16[1,20,128,1024]{3,2,1,0:T(8,128)(2,1)} copy(bf16[1,20,128,1024]{3,1,2,0:T(8,128)(2,1)} %fusion.18) | data formatting | bytes 10485760 | tf_op jit(solution)/shard_map/convert_element_type | solution.py:155
  (41 shorter events, 9.0 us)
Async XLA Ops:
  0.0 39.2 %copy-start = (bf16[16,32,32]{2,1,0:T(8,128)(2,1)S(1)}, bf16[16,32,32]{2,1,0:T(8,128)(2,1)}, u32[]{:S(2)}) copy-start(bf16[16,32,32]{2,1,0:T(8,128)(2,1)} %param.15) | copy-start | bytes 98308
  0.0 65.6 %copy-start.5 = (bf16[32,32,32]{2,1,0:T(8,128)(2,1)S(1)}, bf16[32,32,32]{2,1,0:T(8,128)(2,1)}, u32[]{:S(2)}) copy-start(bf16[32,32,32]{2,1,0:T(8,128)(2,1)} %param.16) | copy-start | bytes 196612
  0.0 133.2 %copy-start.6 = (bf16[20,128]{1,0:T(8,128)(2,1)S(1)}, bf16[20,128]{1,0:T(8,128)(2,1)}, u32[]{:S(2)}) copy-start(bf16[20,128]{1,0:T(8,128)(2,1)} %param.12) | copy-start | bytes 15364
  8.6 123.0 %all-to-all-start = ((bf16[1,1,128,2,128,20]{2,3,5,1,0,4:T(2,128)(2,1)}), bf16[1,1,128,2,128,20]{2,3,5,1,0,4:T(2,128)(2,1)S(1)}, u32[]{:S(2)}, u32[]{:S(2)}) async-start(bf16[1,1,128,2,128,20]{2,3,5,1,0,4:T(2,128)(2,1)} %copy.48), calls=%async_computation | async-start | bytes 2621440 | tf_op jit(solution)/shard_map/all_to_all | solution.py:107
  232.0 47.5 %copy-start.4 = (bf16[128,2,32,32]{2,0,3,1:T(8,128)(2,1)S(1)}, bf16[128,2,32,32]{2,0,3,1:T(8,128)(2,1)}, u32[]{:S(2)}) copy-start(bf16[128,2,32,32]{2,0,3,1:T(8,128)(2,1)} %all_gather.11) | copy-start | bytes 1572868
  279.5 12.2 %copy-start.2 = (f32[1,1024,2,128]{1,3,2,0:T(8,128)S(1)}, f32[1,1024,2,128]{1,3,2,0:T(8,128)}, u32[]{:S(2)}) copy-start(f32[1,1024,2,128]{1,3,2,0:T(8,128)} %get-tuple-element.7) | copy-start | bytes 3145732
  279.5 12.2 %copy-start.3 = (f32[1,1024,2,128]{1,3,2,0:T(8,128)S(1)}, f32[1,1024,2,128]{1,3,2,0:T(8,128)}, u32[]{:S(2)}) copy-start(f32[1,1024,2,128]{1,3,2,0:T(8,128)} %get-tuple-element.8) | copy-start | bytes 3145732
  304.3 98.3 %all-to-all-start.1 = ((bf16[8,1,1,128,2,16,128]{3,6,4,5,2,1,0:T(8,128)(2,1)}), bf16[8,1,1,128,2,16,128]{3,6,4,5,2,1,0:T(8,128)(2,1)}, u32[]{:S(2)}, u32[]{:S(2)}) async-start(bf16[8,1,1,128,2,16,128]{3,6,4,5,2,1,0:T(8,128)(2,1)} %fusion.48), calls=%async_computation.1 | async-start | bytes 16777216 | tf_op jit(solution)/shard_map/all_to_all | solution.py:136
  415.0 26.6 %copy-start.7 = (bf16[128,128]{1,0:T(8,128)(2,1)S(1)}, bf16[128,128]{1,0:T(8,128)(2,1)}, u32[]{:S(2)}) copy-start(bf16[128,128]{1,0:T(8,128)(2,1)} %param.18) | copy-start | bytes 98308
  415.0 26.6 %copy-start.8 = (bf16[128,20]{0,1:T(8,128)(2,1)S(1)}, bf16[128,20]{0,1:T(8,128)(2,1)}, u32[]{:S(2)}) copy-start(bf16[128,20]{0,1:T(8,128)(2,1)} %param.20) | copy-start | bytes 15364
  415.0 26.6 %copy-start.9 = (f32[20]{0:T(128)S(1)}, f32[20]{0:T(128)}, u32[]{:S(2)}) copy-start(f32[20]{0:T(128)} %param.21) | copy-start | bytes 244
  415.0 26.6 %copy-start.10 = (f32[128]{0:T(128)S(1)}, f32[128]{0:T(128)}, u32[]{:S(2)}) copy-start(f32[128]{0:T(128)} %param.19) | copy-start | bytes 1540
  415.1 26.6 %copy-start.11 = (f32[128]{0:T(128)S(1)}, f32[128]{0:T(128)}, u32[]{:S(2)}) copy-start(f32[128]{0:T(128)} %param.13) | copy-start | bytes 1540
  441.7 175.9 %copy-start.1 = (bf16[16,32,32]{2,1,0:T(8,128)(2,1)S(1)}, bf16[16,32,32]{2,1,0:T(8,128)(2,1)}, u32[]{:S(2)}) copy-start(bf16[16,32,32]{2,1,0:T(8,128)(2,1)} %param.15) | copy-start | bytes 98308
